TPU v7x, 32 devices: a whole 2x2x4 slice. The times are simulated.
32 devices in a mesh: groups: 2 (over x), wide: 16 (over z, y, core).
Axes of the slice: x: 2, y: 2, z: 4, core: 2. Of those that a mesh axis runs over, the one named last changes fastest.
Arguments:
- loader_features: bfloat16 [32768, 128], P(('groups', 'wide')), parts along dimension 0, may hold values from -6 to 6
- dest: int32 [32768], P(('groups', 'wide')), parts along dimension 0, may hold values from 0 to 16383, as said below
- block_values: bfloat16 [8192, 128, 128], P(('groups', 'wide')), parts along dimension 0, may hold values from -0.09375 to 0.09375
- row_block: int32 [8192], P(('groups', 'wide')), parts along dimension 0, may hold values from 0 to 7, as said below
- col_block: int32 [8192], P(('groups', 'wide')), parts along dimension 0, may hold values from 0 to 127, as said below
- w_first: bfloat16 [128, 256], replicated, may hold values from -0.5 to 0.5
- b_first: float32 [256], replicated, may hold values from -3 to 3
- w_second: bfloat16 [256, 256], replicated, may hold values from -0.375 to 0.375
- b_second: float32 [256], replicated, may hold values from -3 to 3
Outputs:
- output: bfloat16 [32768, 256], P(('groups', 'wide')), parts along dimension 0
There are 2 independent parts, one for each index of `groups`. A program takes and returns all parts, laid end to end along the dimension named above; an argument that names none is the same for every part. Nothing has to cross between parts.
Inputs may be any that keep to these rules, and one draw needn't show every extreme that they name: dest is a permutation; row i goes to owner dest[i] // 1024. Each device sends at most 256 of its rows to one owner and exactly 256 to some owner; every owner receives exactly 256 rows from some device. `col_block`: A device's list holds 16 groups of 16 entries; in group g every column block lies in device g's nodes (g * 8 to g * 8 + 7); the k-th entry's column block depends only on k mod 2, and these 2 are distinct. `row_block`: in each group, the k-th entry's row block is distinct among entries with the same k mod 2.
All inputs are finite; a program needn't handle non-finite values.
Results may differ from a plain program's by a relative error of at most 0.0058.
Values may be sent and summed in bfloat16 or wider, within the bound.
A program may use at most 128 MiB of HBM per device.

v0:
```python
import math
import jax
import jax.numpy as jnp
from jax import lax
from jax.sharding import PartitionSpec as P


def body(
    loader_features, dest, block_values, row_block, col_block, w_first, b_first, w_second, b_second
):
    devices = lax.axis_size("wide")
    own_index = lax.axis_index("wide")
    node_dev = loader_features.shape[0]
    feature_width = loader_features.shape[1]
    block_size = block_values.shape[1]
    row_blocks = node_dev // block_size
    slots = block_values.shape[0] // devices
    used = slots // row_blocks
    batch_groups = math.gcd(devices, 8)
    all_rows = lax.all_gather(loader_features, "wide", axis=0, tiled=True)
    all_dest = lax.all_gather(dest, "wide", axis=0, tiled=True)
    local = all_dest - own_index * node_dev
    local = jnp.where((local >= 0) & (local < node_dev), local, node_dev)
    features = (
        jnp.zeros((node_dev + 1, feature_width), jnp.bfloat16).at[local].set(all_rows)[:node_dev]
    )
    grid_rows = row_block.reshape(devices, row_blocks, used)
    order = jnp.argsort(grid_rows, axis=1, stable=True)
    grid_values = block_values.reshape(devices, row_blocks, used, block_size, block_size)
    ordered = jnp.take_along_axis(grid_values, order[:, :, :, None, None], axis=1)
    group_cols = col_block.reshape(devices, row_blocks, used)[:, 0, :]

    def aggregate(panel):
        width = panel.shape[1]
        empty = jnp.zeros((row_blocks, block_size, width), jnp.float32)
        carry = empty
        piece = lax.all_gather(panel, "wide", axis=0, tiled=True)
        start = jnp.int32(0)
        length = piece.shape[0]
        tile_count = length // block_size
        piece_tiles = piece.reshape(tile_count, block_size, width)
        first_group = start // node_dev
        covered = -(-length // node_dev) + 0
        covered = min(devices, covered)
        span = min(covered, batch_groups)
        for batch in range(-(-covered // span)):
            wanted_group = first_group + batch * span
            begin = jnp.minimum(wanted_group, devices - span)
            values = lax.dynamic_slice_in_dim(ordered, begin, span, 0)
            cols = lax.dynamic_slice_in_dim(group_cols, begin, span, 0)
            group_of = begin + jnp.arange(span, dtype=jnp.int32)
            valid = (cols >= 0) & (cols < tile_count) & (group_of[:, None] >= wanted_group)
            picked = jnp.take(piece_tiles, jnp.clip(cols, 0, tile_count - 1), axis=0)
            picked = picked * valid.astype(jnp.bfloat16)[:, :, None, None]
            carry = carry + jnp.einsum(
                "gruij,gujw->riw", values, picked, preferred_element_type=jnp.float32
            )
        return carry.reshape(node_dev, width)

    first = aggregate(features).astype(jnp.bfloat16)
    hidden = jax.nn.relu(
        jnp.dot(first, w_first, preferred_element_type=jnp.float32) + b_first
    ).astype(jnp.bfloat16)
    second = aggregate(hidden).astype(jnp.bfloat16)
    output = jnp.dot(second, w_second, preferred_element_type=jnp.float32) + b_second
    return output.astype(jnp.bfloat16)


def solution(mesh):
    placed = (
        P(("groups", "wide"), None),
        P(("groups", "wide")),
        P(("groups", "wide"), None, None),
        P(("groups", "wide")),
        P(("groups", "wide")),
        P(),
        P(),
        P(),
        P(),
    )
    return jax.shard_map(
        body, mesh=mesh, in_specs=placed, out_specs=P(("groups", "wide"), None), check_vma=False
    )
```

profile of v0, /device:TPU:0, one launch (start us, length us, event | category | flops | bytes accessed | tf_op | source)
XLA Modules:
  0.0 262.6 jit_solution(10796248333810704136)
XLA Ops:
  6.5 0.0 copy-start
  6.5 0.0 all-gather.4.cloned.1.call-start
  6.5 0.7 all-gather.4.cloned.1.call-update
  7.3 0.0 all-gather.6.cloned.1.call-start
  7.3 23.6 %all_gather.12 = s32[16384]{0:T(1024)S(1)} all-gather(s32[1024]{0:T(1024)} %param.14), channel_id=1, replica_groups=mesh['groups'=2,'wide'=16] {'wide'}, dimensions={0}, use_global_device_ids=true | all-gather | bytes 69632 | tf_op jit(solution)/shard_map/all_gather | solution.py:21
  31.0 31.9 %all-gather.4.cloned.1.call-done = bf16[16384,128]{1,0:T(8,128)(2,1)} async-done(((bf16[1024,128]{1,0:T(8,128)(2,1)}), bf16[16384,128]{1,0:T(8,128)(2,1)}) %all-gather.4.cloned.1.call-update) | async-done | bytes 4194320 | tf_op jit(solution)/shard_map/all_gather | solution.py:20
  62.9 41.4 %scatter_custom_fusion = bf16[1025,128]{1,0:T(8,128)(2,1)S(1)} fusion(s32[16384]{0:T(1024)S(1)} %compare_select_fusion, bf16[16384,128]{1,0:T(8,128)(2,1)} %all-gather.4.cloned.1.call-done, bf16[]{:T(256)} %constant.78.clone.1), kind=kCustom, calls=%fused_computation.50 | custom fusion | bytes 262912 | tf_op jit(solution)/shard_map/scatter | solution.py:25
  104.3 0.7 slice.22
  105.0 0.0 all-gather.6.cloned.1.call-update
  105.1 0.0 all-gather.8.cloned.1.call-start
  105.1 0.8 reshape.122
  105.9 0.8 reshape.126
  106.8 0.1 copy.79
  106.8 0.1 copy.78
  106.9 0.1 copy.57
  107.1 0.1 copy.62
  107.2 0.1 copy.60
  107.3 0.1 copy.64
  107.4 0.1 copy.59
  107.4 0.1 reshape.189
  107.5 0.1 copy.63
  107.6 0.1 reshape.193
  107.7 5.3 %sort.17 = (s32[16,8,2]{2,1,0:T(8,128)}, s32[16,8,2]{2,1,0:T(8,128)S(1)}) sort(s32[16,8,2]{2,1,0:T(8,128)S(1)} %reshape.122, s32[16,8,2]{2,1,0:T(8,128)S(1)} %iota.16), dimensions={1}, to_apply=%region_0.1 | sort | flops 2048 | bytes 4096 | tf_op jit(solution)/shard_map/jit(argsort)/sort | solution.py:28
  113.0 0.1 reshape.161
  113.1 14.2 %gather_fusion = bf16[256,128,128]{2,1,0:T(8,128)(2,1)} fusion(bf16[16,8,2,128,128]{4,3,2,1,0:T(8,128)(2,1)} %bitcast.79, s32[256]{0:T(256)S(1)} %reshape.161), kind=kCustom, calls=%fused_computation.4 | custom fusion | bytes 16780288 | tf_op jit(solution)/shard_map/jit(take_along_axis)/gather | solution.py:30
  127.4 27.0 %all-gather.6.cloned.1.call-done = bf16[16384,128]{1,0:T(8,128)(2,1)} async-done(((bf16[1024,128]{1,0:T(8,128)(2,1)}), bf16[16384,128]{1,0:T(8,128)(2,1)}) %all-gather.6.cloned.1.call-update) | async-done | bytes 4194320 | tf_op jit(solution)/shard_map/all_gather | solution.py:37
  154.4 2.8 %gather_fusion.1 = bf16[16,128,128]{2,1,0:T(8,128)(2,1)S(1)} fusion(bf16[128,128,128]{2,1,0:T(8,128)(2,1)} %bitcast.93, s32[1024]{0:T(1024)S(1)} %pad_clamp_fusion.1), kind=kCustom, calls=%fused_computation.clone | custom fusion | bytes 1048640 | tf_op jit(solution)/shard_map/jit(_take)/gather | solution.py:53
  157.3 2.8 %gather_fusion.2 = bf16[16,128,128]{2,1,0:T(8,128)(2,1)S(1)} fusion(bf16[128,128,128]{2,1,0:T(8,128)(2,1)} %bitcast.94, s32[1024]{0:T(1024)S(1)} %pad_clamp_fusion), kind=kCustom, calls=%fused_computation.2.clone | custom fusion | bytes 1048640 | tf_op jit(solution)/shard_map/jit(_take)/gather | solution.py:53
  160.1 0.0 copy-start.1
  160.1 0.0 copy-start.2
  160.1 0.0 copy-start.3
  160.1 3.7 %fusion.15 = f32[8,128,128]{2,1,0:T(8,128)S(1)} fusion(bf16[16,8,2,128,128]{4,3,2,1,0:T(8,128)(2,1)} %bitcast.80, pred[16,8,2]{2,1,0:T(8,128)(4,1)S(1)} %compare_and_fusion, bf16[8,2,128,128]{3,2,1,0:T(8,128)(2,1)S(1)} %bitcast.91, pred[8,2]{1,0:T(8,128)(4,1)S(1)} %copy.57, bf16[8,2]{1,0:T(8,128)(2,1)S(1)} %copy.60), kind=kOutput, calls=%fused_computation.24 | convolution fusion | flops 542375936 | bytes 9437488 | tf_op jit(solution)/shard_map/gruij,gujw->riw/dot_general | solution.py:55
  163.8 0.9 copy-done.1
  164.8 1.4 fusion.18
  166.1 0.0 copy-done.2
  166.1 0.0 copy-done.3
  166.2 1.1 fusion.13
  167.2 0.0 all-gather.8.cloned.1.call-update
  167.3 73.5 %all-gather.8.cloned.1.call-done = bf16[16384,256]{1,0:T(8,128)(2,1)} async-done(((bf16[1024,256]{1,0:T(8,128)(2,1)}), bf16[16384,256]{1,0:T(8,128)(2,1)}) %all-gather.8.cloned.1.call-update) | async-done | bytes 8388624 | tf_op jit(solution)/shard_map/all_gather | solution.py:37
  240.8 4.0 %gather_fusion.4 = bf16[16,128,256]{2,1,0:T(8,128)(2,1)S(1)} fusion(bf16[128,128,256]{2,1,0:T(8,128)(2,1)} %bitcast.88, s32[1024]{0:T(1024)S(1)} %pad_clamp_fusion), kind=kCustom, calls=%fused_computation.3.clone | custom fusion | bytes 2097216 | tf_op jit(solution)/shard_map/jit(_take)/gather | solution.py:53
  244.8 4.0 %gather_fusion.3 = bf16[16,128,256]{2,1,0:T(8,128)(2,1)S(1)} fusion(bf16[128,128,256]{2,1,0:T(8,128)(2,1)} %bitcast.89, s32[1024]{0:T(1024)S(1)} %pad_clamp_fusion.1), kind=kCustom, calls=%fused_computation.1.clone | custom fusion | bytes 2097216 | tf_op jit(solution)/shard_map/jit(_take)/gather | solution.py:53
  248.8 0.0 slice-start
  248.8 0.0 slice-start.1
  248.8 3.7 %fusion.8 = f32[8,128,256]{2,1,0:T(8,128)S(1)} fusion(bf16[16,8,2,128,128]{4,3,2,1,0:T(8,128)(2,1)} %bitcast.81, pred[16,8,2]{2,1,0:T(8,128)(4,1)S(1)} %compare_and_fusion, bf16[8,2,128,256]{3,2,1,0:T(8,128)(2,1)S(1)} %bitcast.87, pred[8,2]{1,0:T(8,128)(4,1)S(1)} %copy.57, bf16[8,2]{1,0:T(8,128)(2,1)S(1)} %copy.60), kind=kOutput, calls=%fused_computation.15 | convolution fusion | flops 1080557568 | bytes 10486064 | tf_op jit(solution)/shard_map/gruij,gujw->riw/dot_general | solution.py:55
  252.6 0.0 slice-done
  252.6 1.0 slice-done.1
  253.5 0.0 copy-start.4
  253.5 1.4 fusion.12
  255.0 0.0 copy-done
  255.0 0.0 copy-done.4
  255.0 1.1 fusion.14
  (14 shorter events, 0.1 us)
Async XLA Ops:
  6.5 248.4 %copy-start = (bf16[256,256]{1,0:T(8,128)(2,1)S(1)}, bf16[256,256]{1,0:T(8,128)(2,1)}, u32[]{:S(2)}) copy-start(bf16[256,256]{1,0:T(8,128)(2,1)} %param.20) | copy-start | bytes 393220
  6.5 56.4 %all-gather.4.cloned.1.call-start = ((), (), s32[]{:S(2)}) async-start(), calls=%async_computation | async-start | bytes 4456448 | tf_op jit(solution)/shard_map/all_gather | solution.py:20
  7.3 147.2 %all-gather.6.cloned.1.call-start = ((), (), s32[]{:S(2)}) async-start(), calls=%async_computation.1 | async-start | bytes 4456448 | tf_op jit(solution)/shard_map/all_gather | solution.py:37
  105.1 135.8 %all-gather.8.cloned.1.call-start = ((), (), s32[]{:S(2)}) async-start(), calls=%async_computation.2 | async-start | bytes 8912896 | tf_op jit(solution)/shard_map/all_gather | solution.py:37
  160.1 4.6 %copy-start.1 = (bf16[256,128,128]{2,1,0:T(8,128)(2,1)S(1)}, bf16[256,128,128]{2,1,0:T(8,128)(2,1)}, u32[]{:S(2)}) copy-start(bf16[256,128,128]{2,1,0:T(8,128)(2,1)} %gather_fusion) | copy-start | bytes 25165828
  160.1 6.0 %copy-start.2 = (bf16[128,256]{1,0:T(8,128)(2,1)S(1)}, bf16[128,256]{1,0:T(8,128)(2,1)}, u32[]{:S(2)}) copy-start(bf16[128,256]{1,0:T(8,128)(2,1)} %param.18) | copy-start | bytes 196612
  160.1 6.0 %copy-start.3 = (f32[256]{0:T(256)S(1)}, f32[256]{0:T(256)}, u32[]{:S(2)}) copy-start(f32[256]{0:T(256)} %param.19) | copy-start | bytes 3076
  248.8 3.8 %slice-start = ((s8[8388608]{0:T(1024)(128)(4,1)}), s8[4194304]{0:T(1024)(128)(4,1)S(1)}, s32[]{:S(2)}) async-start(s8[8388608]{0:T(1024)(128)(4,1)} %bitcast.83), calls=%async_computation.3 | async-start | bytes 8388608
  248.8 4.7 %slice-start.1 = ((s8[8388608]{0:T(1024)(128)(4,1)}), s8[4194304]{0:T(1024)(128)(4,1)S(1)}, s32[]{:S(2)}) async-start(s8[8388608]{0:T(1024)(128)(4,1)} %bitcast.83), calls=%async_computation.4 | async-start | bytes 8388608
  253.5 1.4 copy-start.4
Sparse Core Ops, SparseCore 0:
  9.5 53.3 all-gather.3
  105.2 49.2 all-gather.5
  167.4 73.3 all-gather.7
where the time goes:
time: 263 us
  waiting for transfers between devices  133 us (51%)
  local copies, waits for them, and re-layouts  74.5 us (28%)
  blocking collectives  23.6 us (9%)
  between operations  13.3 us (5%)
  matrix products  12.4 us (5%)
  other arithmetic  5.39 us (2%)
    all_gather x2, waiting for transfers between devices, aggregate(): piece = lax.all_gather(panel, 'wide', axis=0, tiled=True)  101 us
    scatter x1, local copies, waits for them, and re-layouts, body(): jnp.zeros((node_dev + 1, feature_width), jnp.bfloat16).at[local]  41.4 us
    all_gather x1, waiting for transfers between devices, body(): all_rows = lax.all_gather(loader_features, 'wide', axis=0, tiled=True)  31.9 us
    all_gather x1, blocking collectives, body(): all_dest = lax.all_gather(dest, 'wide', axis=0, tiled=True)  23.6 us
    gather x2, local copies, waits for them, and re-layouts, body(): jnp.take_along_axis(grid_values, order[:, :, :, None, None], axis=1)  14.3 us
    gather x4, local copies, waits for them, and re-layouts, aggregate(): picked = jnp.take(piece_tiles, jnp.clip(cols, 0, tile_count - 1), axis=0)  13.7 us
    dot_general x4, matrix products, aggregate(): jnp.einsum('gruij,gujw->riw', values, picked, preferred_element_type=jnp....  10.2 us
    sort x1, other arithmetic, body(): order = jnp.argsort(grid_rows, axis=1, stable=True)  5.26 us
  transfers between devices with their start and end apart: 3, of which 3 were waited for; matrix products, arithmetic and copies ran while one was open for 8% of the time, Pallas kernels for 0%

commit v1 on v0

--- a/solution.py
+++ b/solution.py
@@ -17,7 +17,14 @@
     slots = block_values.shape[0] // devices
     used = slots // row_blocks
     batch_groups = math.gcd(devices, 8)
-    all_rows = lax.all_gather(loader_features, "wide", axis=0, tiled=True)
+    ways, here = (lax.axis_size("wide"), lax.axis_index("wide"))
+    all_rows, reach = (loader_features, 1)
+    while reach < ways:
+        theirs = lax.ppermute(all_rows, "wide", [(d, d ^ reach) for d in range(ways)])
+        mine_first = jnp.concatenate([all_rows, theirs], axis=0)
+        theirs_first = jnp.concatenate([theirs, all_rows], axis=0)
+        all_rows = jnp.where(here & reach == 0, mine_first, theirs_first)
+        reach = 2 * reach
     all_dest = lax.all_gather(dest, "wide", axis=0, tiled=True)
     local = all_dest - own_index * node_dev
     local = jnp.where((local >= 0) & (local < node_dev), local, node_dev)

time: 263 us -> 371 us (1.41)
  other arithmetic: 5.39 us -> 64.8 us
  waiting for transfers between devices: 133 us -> 180 us
  local copies, waits for them, and re-layouts: 74.5 us -> 30.8 us
  blocking collectives: 23.6 us -> 59.4 us
  starting transfers between devices: 0.08 us -> 8.05 us
    ppermute x0 -> x4, waiting for transfers between devices: none -> 67 us  [body(): lax.ppermute(all_rows, 'wide', [(d, d ^ reach) for d in range(ways)])]
    scatter x0 -> x1, other arithmetic: none -> 55.9 us  [body(): jnp.zeros((node_dev + 1, feature_width), jnp.bfloat16).at[local]]
    scatter x1 -> x0, local copies, waits for them, and re-layouts: 41.4 us -> none  [body(): jnp.zeros((node_dev + 1, feature_width), jnp.bfloat16).at[local]]
    all_gather x1, blocking collectives: 23.6 us -> 59.4 us  [body(): all_dest = lax.all_gather(dest, 'wide', axis=0, tiled=True)]
    all_gather x1 -> x0, waiting for transfers between devices: 31.9 us -> none  [body(): all_rows = lax.all_gather(loader_features, 'wide', axis=0, tiled=True)]
    all_gather x2, waiting for transfers between devices: 101 us -> 113 us  [aggregate(): piece = lax.all_gather(panel, 'wide', axis=0, tiled=True)]
    ppermute x0 -> x4, starting transfers between devices: none -> 7.82 us  [body(): lax.ppermute(all_rows, 'wide', [(d, d ^ reach) for d in range(ways)])]
  transfers between devices with their start and end apart: 3 -> 6, of which waited for: 3 -> 6; matrix products, arithmetic and copies ran while one was open for 8% -> 6% of each run, Pallas kernels for 0% -> 0%
where the time goes in v1:
time: 371 us
  waiting for transfers between devices  180 us (49%)
  other arithmetic  64.8 us (17%)
  blocking collectives  59.4 us (16%)
  local copies, waits for them, and re-layouts  30.8 us (8%)
  matrix products  14.4 us (4%)
  between operations  13.6 us (4%)
  starting transfers between devices  8.05 us (2%)
    all_gather x2, waiting for transfers between devices, aggregate(): piece = lax.all_gather(panel, 'wide', axis=0, tiled=True)  113 us
    ppermute x4, waiting for transfers between devices, body(): lax.ppermute(all_rows, 'wide', [(d, d ^ reach) for d in range(ways)])  67 us
    all_gather x1, blocking collectives, body(): all_dest = lax.all_gather(dest, 'wide', axis=0, tiled=True)  59.4 us
    scatter x1, other arithmetic, body(): jnp.zeros((node_dev + 1, feature_width), jnp.bfloat16).at[local]  55.9 us
    gather x2, local copies, waits for them, and re-layouts, body(): jnp.take_along_axis(grid_values, order[:, :, :, None, None], axis=1)  14.3 us
    gather x4, local copies, waits for them, and re-layouts, aggregate(): picked = jnp.take(piece_tiles, jnp.clip(cols, 0, tile_count - 1), axis=0)  13.7 us
    dot_general x4, matrix products, aggregate(): jnp.einsum('gruij,gujw->riw', values, picked, preferred_element_type=jnp....  12.3 us
    ppermute x4, starting transfers between devices, body(): lax.ppermute(all_rows, 'wide', [(d, d ^ reach) for d in range(ways)])  7.82 us
  transfers between devices with their start and end apart: 6, of which 6 were waited for; matrix products, arithmetic and copies ran while one was open for 6% of the time, Pallas kernels for 0%

profile of v1, /device:TPU:0, one launch (start us, length us, event | category | flops | bytes accessed | tf_op | source)
XLA Modules:
  0.0 371.0 jit_solution(17542973434701372186)
XLA Ops:
  6.5 0.0 copy-start
  6.5 0.0 copy-start.3
  6.5 0.0 all-gather.3.cloned.1.call-start
  6.5 0.5 collective-permute-start
  7.0 1.4 collective-permute-done
  8.4 1.2 maximum_select_fusion.4
  9.6 3.0 collective-permute-start.1
  12.5 12.2 %collective-permute-done.1 = bf16[2048,128]{1,0:T(8,128)(2,1)S(1)} collective-permute-done((bf16[2048,128]{1,0:T(8,128)(2,1)S(1)}, bf16[2048,128]{1,0:T(8,128)(2,1)S(1)}, u32[]{:S(2)}, u32[]{:S(2)}) %collective-permute-start.1) | collective-permute-done | bytes 524320 | tf_op jit(solution)/shard_map/ppermute | solution.py:23
  24.8 0.3 maximum_select_fusion.3
  25.0 1.9 collective-permute-start.2
  26.9 0.0 copy-start.4
  26.9 0.0 copy-start.5
  26.9 23.0 %collective-permute-done.2 = bf16[4096,128]{1,0:T(8,128)(2,1)} collective-permute-done((bf16[4096,128]{1,0:T(8,128)(2,1)S(1)}, bf16[4096,128]{1,0:T(8,128)(2,1)}, u32[]{:S(2)}, u32[]{:S(2)}) %collective-permute-start.2) | collective-permute-done | bytes 1048608 | tf_op jit(solution)/shard_map/ppermute | solution.py:23
  49.9 2.1 maximum_select_fusion.2
  52.0 2.6 collective-permute-start.3
  54.5 0.0 copy-done.3
  54.5 59.4 %all_gather.9 = s32[16384]{0:T(1024)S(1)} all-gather(s32[1024]{0:T(1024)S(1)} %copy-done.3), channel_id=1, replica_groups=mesh['groups'=2,'wide'=16] {'wide'}, dimensions={0}, use_global_device_ids=true | all-gather | bytes 69632 | tf_op jit(solution)/shard_map/all_gather | solution.py:28
  114.0 30.4 %collective-permute-done.3 = bf16[8192,128]{1,0:T(8,128)(2,1)} collective-permute-done((bf16[8192,128]{1,0:T(8,128)(2,1)S(1)}, bf16[8192,128]{1,0:T(8,128)(2,1)}, u32[]{:S(2)}, u32[]{:S(2)}) %collective-permute-start.3) | collective-permute-done | bytes 2097184 | tf_op jit(solution)/shard_map/ppermute | solution.py:23
  144.3 55.9 %scatter_custom_fusion = bf16[1025,128]{1,0:T(8,128)(2,1)S(1)} fusion(s32[16384]{0:T(1024)S(1)} %compare_select_fusion, bf16[8192,128]{1,0:T(8,128)(2,1)} %collective-permute-done.3, bf16[]{:T(256)} %constant.110, bf16[8192,128]{1,0:T(8,128)(2,1)S(1)} %maximum_select_fusion.2, pred[]{:T(512)S(6)} %eq.12, bf16[]{:T(256)} %constant.81.clone.1), kind=kCustom, calls=%fused_computation.12 | custom fusion | flops 18874368 | bytes 4456709 | tf_op jit(solution)/shard_map/scatter | solution.py:32
  200.2 0.7 slice.22
  201.0 0.0 all-gather.3.cloned.1.call-update
  201.0 0.2 all-gather.5.cloned.1.call-start
  201.2 0.0 copy-done.4
  201.2 0.1 reshape.122
  201.4 0.0 copy-done.5
  201.4 0.1 reshape.126
  201.5 0.1 copy.79
  201.6 0.1 copy.78
  201.7 0.1 copy.57
  201.8 0.1 copy.62
  201.9 0.1 copy.60
  202.0 0.1 copy.64
  202.1 0.1 copy.59
  202.2 0.1 reshape.189
  202.3 0.1 copy.63
  202.4 0.1 reshape.193
  202.5 5.3 %sort.17 = (s32[16,8,2]{2,1,0:T(8,128)}, s32[16,8,2]{2,1,0:T(8,128)S(1)}) sort(s32[16,8,2]{2,1,0:T(8,128)S(1)} %reshape.122, s32[16,8,2]{2,1,0:T(8,128)S(1)} %iota.16), dimensions={1}, to_apply=%region_0.1 | sort | flops 2048 | bytes 4096 | tf_op jit(solution)/shard_map/jit(argsort)/sort | solution.py:35
  207.8 0.1 reshape.161
  207.9 14.2 %gather_fusion = bf16[256,128,128]{2,1,0:T(8,128)(2,1)} fusion(bf16[16,8,2,128,128]{4,3,2,1,0:T(8,128)(2,1)} %bitcast.79, s32[256]{0:T(256)S(1)} %reshape.161), kind=kCustom, calls=%fused_computation.4 | custom fusion | bytes 16780288 | tf_op jit(solution)/shard_map/jit(take_along_axis)/gather | solution.py:37
  222.1 39.3 %all-gather.3.cloned.1.call-done = bf16[16384,128]{1,0:T(8,128)(2,1)} async-done(((bf16[1024,128]{1,0:T(8,128)(2,1)}), bf16[16384,128]{1,0:T(8,128)(2,1)}) %all-gather.3.cloned.1.call-update) | async-done | bytes 4194320 | tf_op jit(solution)/shard_map/all_gather | solution.py:44
  261.5 2.8 gather_fusion.2
  264.3 2.8 gather_fusion.1
  267.2 0.0 copy-start.1
  267.2 3.7 fusion.22
  270.9 0.9 copy-done.1
  271.8 0.0 copy-start.2
  271.8 0.0 copy-start.6
  271.8 1.4 fusion.25
  273.2 0.0 copy-done.2
  273.2 0.0 copy-done.6
  273.2 1.1 fusion.20
  274.3 0.0 all-gather.5.cloned.1.call-update
  274.3 73.5 %all-gather.5.cloned.1.call-done = bf16[16384,256]{1,0:T(8,128)(2,1)} async-done(((bf16[1024,256]{1,0:T(8,128)(2,1)}), bf16[16384,256]{1,0:T(8,128)(2,1)}) %all-gather.5.cloned.1.call-update) | async-done | bytes 8388624 | tf_op jit(solution)/shard_map/all_gather | solution.py:44
  347.9 4.0 %gather_fusion.4 = bf16[16,128,256]{2,1,0:T(8,128)(2,1)S(1)} fusion(bf16[128,128,256]{2,1,0:T(8,128)(2,1)} %bitcast.86, s32[1024]{0:T(1024)S(1)} %pad_clamp_fusion), kind=kCustom, calls=%fused_computation.3.clone | custom fusion | bytes 2097216 | tf_op jit(solution)/shard_map/jit(_take)/gather | solution.py:60
  351.9 4.0 %gather_fusion.3 = bf16[16,128,256]{2,1,0:T(8,128)(2,1)S(1)} fusion(bf16[128,128,256]{2,1,0:T(8,128)(2,1)} %bitcast.87, s32[1024]{0:T(1024)S(1)} %pad_clamp_fusion.1), kind=kCustom, calls=%fused_computation.1.clone | custom fusion | bytes 2097216 | tf_op jit(solution)/shard_map/jit(_take)/gather | solution.py:60
  355.9 3.6 fusion.15
  359.5 0.0 copy-start.7
  359.5 3.6 fusion.19
  363.1 0.0 copy-done
  363.1 0.0 copy-done.7
  363.1 1.1 fusion.21
  (13 shorter events, 0.1 us)
Async XLA Ops:
  6.5 356.5 %copy-start = (bf16[256,256]{1,0:T(8,128)(2,1)S(1)}, bf16[256,256]{1,0:T(8,128)(2,1)}, u32[]{:S(2)}) copy-start(bf16[256,256]{1,0:T(8,128)(2,1)} %param.20) | copy-start | bytes 393220
  6.5 48.0 %copy-start.3 = (s32[1024]{0:T(1024)S(1)}, s32[1024]{0:T(1024)}, u32[]{:S(2)}) copy-start(s32[1024]{0:T(1024)} %param.14) | copy-start | bytes 12292
  6.5 254.9 %all-gather.3.cloned.1.call-start = ((), (), s32[]{:S(2)}) async-start(), calls=%async_computation | async-start | bytes 4456448 | tf_op jit(solution)/shard_map/all_gather | solution.py:44
  6.5 1.8 collective-permute-start
  9.6 15.2 %collective-permute-start.1 = (bf16[2048,128]{1,0:T(8,128)(2,1)S(1)}, bf16[2048,128]{1,0:T(8,128)(2,1)S(1)}, u32[]{:S(2)}, u32[]{:S(2)}) collective-permute-start(bf16[2048,128]{1,0:T(8,128)(2,1)S(1)} %maximum_select_fusion.4), channel_id=1, source_target_pairs={{0,2},{1,3},{2,0},{3,1},{4,6},{5,7},{6,4},{7,5},{8,10},{9,11},{10,... | collective-permute-start | bytes 1572872 | tf_op jit(solution)/shard_map/ppermute | solution.py:23
  25.0 24.9 %collective-permute-start.2 = (bf16[4096,128]{1,0:T(8,128)(2,1)S(1)}, bf16[4096,128]{1,0:T(8,128)(2,1)}, u32[]{:S(2)}, u32[]{:S(2)}) collective-permute-start(bf16[4096,128]{1,0:T(8,128)(2,1)S(1)} %maximum_select_fusion.3), channel_id=1, source_target_pairs={{0,4},{1,5},{2,6},{3,7},{4,0},{5,1},{6,2},{7,3},{8,12},{9,13},{10,... | collective-permute-start | bytes 3145736 | tf_op jit(solution)/shard_map/ppermute | solution.py:23
  26.9 174.3 %copy-start.4 = (s32[256]{0:T(256)S(1)}, s32[256]{0:T(256)}, u32[]{:S(2)}) copy-start(s32[256]{0:T(256)} %param.16) | copy-start | bytes 3076
  26.9 174.5 %copy-start.5 = (s32[256]{0:T(256)S(1)}, s32[256]{0:T(256)}, u32[]{:S(2)}) copy-start(s32[256]{0:T(256)} %param.17) | copy-start | bytes 3076
  52.0 92.4 %collective-permute-start.3 = (bf16[8192,128]{1,0:T(8,128)(2,1)S(1)}, bf16[8192,128]{1,0:T(8,128)(2,1)}, u32[]{:S(2)}, u32[]{:S(2)}) collective-permute-start(bf16[8192,128]{1,0:T(8,128)(2,1)S(1)} %maximum_select_fusion.2), channel_id=1, source_target_pairs={{0,8},{1,9},{2,10},{3,11},{4,12},{5,13},{6,14},{7,15},{8,0},{9,1},... | collective-permute-start | bytes 6291464 | tf_op jit(solution)/shard_map/ppermute | solution.py:23
  201.0 146.9 %all-gather.5.cloned.1.call-start = ((), (), s32[]{:S(2)}) async-start(), calls=%async_computation.1 | async-start | bytes 8912896 | tf_op jit(solution)/shard_map/all_gather | solution.py:44
  267.2 4.6 %copy-start.1 = (bf16[256,128,128]{2,1,0:T(8,128)(2,1)S(1)}, bf16[256,128,128]{2,1,0:T(8,128)(2,1)}, u32[]{:S(2)}) copy-start(bf16[256,128,128]{2,1,0:T(8,128)(2,1)} %gather_fusion) | copy-start | bytes 25165828
  271.8 1.4 copy-start.2
  271.8 1.4 copy-start.6
  359.5 3.6 copy-start.7
Sparse Core Ops, SparseCore 0:
  201.1 60.3 all-gather.2
  274.4 73.3 all-gather.4
